TPU v7x, 256 devices: a whole 4x4x8 slice. The times are simulated.
256 devices in a mesh: gx: 8 (over x, core), gy: 8 (over y, z_hi), gz: 4 (over z_lo).
Axes of the slice: x: 4, y: 4, z: 8 (z_hi: 2, z_lo: 4; z = z_hi * 4 + z_lo), core: 2. Of those that a mesh axis runs over, the one named last changes fastest.
Arguments:
- patches: bfloat16 [320, 5120], P(('gy', 'gz'), 'gx'), may hold values from -6 to 6
- merge_inner: bfloat16 [5120, 5120], P('gx', ('gy', 'gz')), may hold values from -0.078125 to 0.078125
- merge_outer: bfloat16 [5120, 8192], P(('gy', 'gz'), 'gx'), may hold values from -0.078125 to 0.078125
- gate_weight: bfloat16 [8192, 28672], P('gx', ('gy', 'gz')), may hold values from -0.0625 to 0.0625
- up_weight: bfloat16 [8192, 28672], P('gx', ('gy', 'gz')), may hold values from -0.0625 to 0.0625
- down_weight: bfloat16 [28672, 8192], P(('gy', 'gz'), 'gx'), may hold values from -0.03125 to 0.03125
- out_grad: bfloat16 [320, 8192], P(('gy', 'gz'), 'gx'), may hold values from -1.5 to 1.5
Outputs:
- patch_grad: bfloat16 [320, 5120], P(None, 'gx')
- inner_grad: bfloat16 [5120, 5120], P('gx', ('gy', 'gz'))
- outer_grad: bfloat16 [5120, 8192], P(('gy', 'gz'), 'gx')
- gate_grad: bfloat16 [8192, 28672], P('gx', ('gy', 'gz'))
- up_grad: bfloat16 [8192, 28672], P('gx', ('gy', 'gz'))
- down_grad: bfloat16 [28672, 8192], P(('gy', 'gz'), 'gx')
All inputs are finite; a program needn't handle non-finite values.
Results may differ from a plain program's by a relative error of at most 0.015.
Values may be sent and summed in bfloat16 or wider, within the bound.
A program may use at most 64 MiB of HBM per device.

v0:
```python
import jax
import jax.numpy as jnp
from jax import lax
from jax.experimental import pallas as pl
from jax.experimental.pallas import tpu as pltpu
from jax.sharding import PartitionSpec as P

MESH = pl.DeviceIdType.MESH
F32 = jnp.float32
BF16 = jnp.bfloat16
NX, NY, NZ = 4, 4, 8
ROWS = 80
LANES = 128
OWN, REST = 512, 384


def gelu_parts(pre_act):
    normal_cdf = 0.5 * (1.0 + lax.erf(pre_act * 0.7071067811865476))
    normal_pdf = jnp.exp(-0.5 * pre_act * pre_act) * 0.3989422804014327
    return (pre_act * normal_cdf, normal_cdf + pre_act * normal_pdf)


def swiglu_backward(gate_sum, up_sum, down_sum):
    logistic = jax.nn.sigmoid(gate_sum)
    swish_value = gate_sum * logistic
    swish_slope = logistic * (1.0 + gate_sum * (1.0 - logistic))
    hidden = (swish_value * up_sum).astype(BF16)
    gate_in = (down_sum * up_sum * swish_slope).astype(BF16)
    up_in = (down_sum * swish_value).astype(BF16)
    return (hidden, gate_in, up_in)


def dot(left, right):
    return jnp.dot(left, right, preferred_element_type=F32)


def dot_back(left, right):
    return lax.dot_general(left, right, (((1,), (1,)), ((), ())), preferred_element_type=F32)


def dot_tokens(left, right):
    return lax.dot_general(left, right, (((0,), (0,)), ((), ())), preferred_element_type=F32)


def at(start, size, unit):
    return pl.ds(pl.multiple_of(start, unit), size)


SCRATCH = dict(
    wi=((640, 640), BF16), wo=((640, 1024), BF16), wg=((1024, 896), BF16), wu=((1024, 896), BF16), wd=((896, 1024), BF16),
    p10=((10, 640), BF16), o10=((10, 1024), BF16), pp=((16, 640), BF16), op=((16, 1024), BF16),
    pz=((128, 640), BF16), oz=((128, 1024), BF16), pf=((NY, ROWS, 640), BF16), of=((NY, ROWS, 1024), BF16),
    dp=((NX, ROWS, 896), BF16), dc=((NX, ROWS, OWN), BF16), d1=((NX, ROWS, OWN), BF16), dx=((3, ROWS, OWN), BF16),
    dsum=((ROWS, OWN), F32),
)
PARTS = ((0, 48), (48, 32))
Z_FIRST = (0, 48)


def part_scratch(r):
    return dict(
        ax=((NX, r, 640), BF16), a1=((r, 640), BF16), a2=((r, 640), BF16), slope=((r, 640), F32),
        hs=((NY, r, 160), BF16), hr=((NY, r, 160), BF16),
        ms=((r, 1024), BF16), mz=((7, r, LANES), BF16), m1=((r, LANES), BF16), mf=((NY, r, 1024), BF16),
        gp=((NX, r, 896), BF16), gc=((NX, r, OWN), BF16),
        up=((NX, r, 896), BF16), uc=((NX, r, OWN), BF16), gu=((NX, r, 2 * OWN), BF16), gux=((3, r, 2 * OWN), BF16),
        io=((NX, r, 2 * OWN), BF16), gir=((NX, r, REST), BF16), uir=((NX, r, REST), BF16),
        hdo=((NX, r, OWN), BF16), hdr=((NX, r, REST), BF16),
        bp=((NY, r, 1024), BF16), by=((3, r, 1024), BF16), bs=((r, 1024), BF16),
        bz=((7, r, LANES), BF16), b1=((r, LANES), BF16), bf=((NY, r, 1024), BF16),
        cx=((NX, r, 640), BF16), c1=((r, 640), BF16), c2=((r, 640), BF16), pg=((r, 640), BF16),
        gs=((NY, r, 160), BF16), gr=((NY, r, 160), BF16),
        qs=((r, 640), BF16), qz=((7, r, LANES), BF16), q1=((r, LANES), BF16),
    )


SEMS = 320
OWNERS = 5


class Refs:
    pass


def kernel(*refs):
    patches, grads, wi_in, wo_in, wg_in, wu_in, wd_in = refs[:7]
    s = Refs()
    s.qf, s.ig, s.og, s.gg, s.ug, s.dg = refs[7:13]
    names = iter(refs[13:-3])
    for name in SCRATCH:
        setattr(s, name, next(names))
    halves_of = [Refs() for _ in PARTS]
    for t, (_, r) in zip(halves_of, PARTS):
        for name in part_scratch(r):
            setattr(t, name, next(names))
    send_sems, recv_sems, local_sems = refs[-3:]
    gx, gy, gz = lax.axis_index("gx"), lax.axis_index("gy"), lax.axis_index("gz")
    x, c = gx // 2, gx % 2
    y, z = gy // 2, (gy % 2) * 4 + gz
    ring = (2, 1, 3)
    ring_z = (4, 3, 5, 2, 6, 1, 7)
    to_y = [((y + d) % NY, (gx, ((y + d) % NY) * 2 + z // 4, gz)) for d in ring]
    to_x = [((x + d) % NX, (((x + d) % NX) * 2 + c, gy, gz)) for d in ring]
    to_z = [((z + d) % NZ, (gx, y * 2 + ((z + d) % NZ) // 4, ((z + d) % NZ) % 4)) for d in ring_z]
    to_c = (x * 2 + (1 - c), gy, gz)

    started = []
    count = [0, 0]

    def plan(src, dst, device):
        i = count[0]
        count[0] += 1
        return pltpu.make_async_remote_copy(
            src_ref=src, dst_ref=dst, send_sem=send_sems.at[i], recv_sem=recv_sems.at[i], device_id=device, device_id_type=MESH
        )

    def send(src, dst, device):
        copy = plan(src, dst, device)
        copy.start()
        started.append(copy.wait_send)
        return copy

    def move(src, dst):
        copy = pltpu.make_async_copy(src, dst, local_sems.at[count[1]])
        count[1] += 1
        copy.start()
        return copy

    def arrive(copies):
        for copy in copies:
            copy.wait_recv()

    def cols(i):
        return at(i * LANES, LANES, LANES)

    def scatter_blocks(src, dst, peers, part=slice(None)):
        return [send(src.at[p, :, part], dst.at[k, :, part], device) for k, (p, device) in enumerate(peers)]

    def spread(ref, peers):
        return [send(ref, ref, device) for _, device in peers]

    def scatter_cols(src, dst):
        return [send(src.at[:, cols(p)], dst.at[k], device) for k, (p, device) in enumerate(to_z)]

    def total(own, parts):
        value = own.astype(F32)
        for k in range(parts.shape[0]):
            value = value + parts[k].astype(F32)
        return value

    def in_order(parts):
        return total(parts[0], parts.at[1:])

    def tiles(total_cols, fn):
        full = total_cols // 256

        def step(t, carry):
            fn(pl.multiple_of(t * 256, 256), 256)
            return carry

        lax.fori_loop(0, full, step, 0)
        if total_cols % 256:
            fn(full * 256, total_cols % 256)

    strip = at(y * 160, 160, 16)
    loads = {n: move(r, d) for n, r, d in (
        ("patches", patches, s.p10), ("grads", grads, s.o10),
        ("wi", wi_in, s.wi.at[strip]), ("wo", wo_in, s.wo.at[strip]), ("wd", wd_in, s.wd), ("wg", wg_in, s.wg), ("wu", wu_in, s.wu)
    )}

    barrier = pltpu.get_barrier_semaphore()
    peers = [d for _, d in to_z + to_y + to_x] + [to_c]
    for device in peers:
        pl.semaphore_signal(barrier, inc=1, device_id=device, device_id_type=MESH)

    deal = (lax.broadcasted_iota(jnp.int32, (16, 10), 0) == lax.broadcasted_iota(jnp.int32, (16, 10), 1)).astype(F32).astype(BF16)
    loads["patches"].wait()
    s.pp[...] = dot(deal, s.p10[...]).astype(BF16)
    loads["grads"].wait()
    s.op[...] = dot(deal, s.o10[...]).astype(BF16)
    row = lax.broadcasted_iota(jnp.int32, (ROWS, 128), 0)
    col = lax.broadcasted_iota(jnp.int32, (ROWS, 128), 1)
    pick = jnp.where(col == row + 6 * ((row * 205) >> 11), 1.0, 0.0).astype(BF16)
    pl.semaphore_wait(barrier, len(peers))

    def gather_z(src, buf):
        copies = [send(src, buf.at[at(z * 16, 16, 16)], device) for _, device in to_z]
        buf[at(z * 16, 16, 16), :] = src[...]
        return copies

    p_z = gather_z(s.pp, s.pz)
    loads["wi"].wait()
    wi_y = spread(s.wi.at[strip], to_y[1:])
    arrive(p_z)
    s.pf[y] = dot(pick, s.pz[...]).astype(BF16)

    def pass_on(buf, copies):
        halves = [at((y + d) % NY * 160 + h, 80, 16) for d, h in ((3, 0), (1, 80))]
        arrive(copies)
        return [send(buf.at[half], buf.at[half], device) for half, (_, device) in zip(halves, to_y[1:])]

    wi_y = pass_on(s.wi, wi_y)
    o_z = gather_z(s.op, s.oz)
    loads["wo"].wait()
    wo_y = spread(s.wo.at[strip], to_y[1:])
    arrive(wi_y)

    mine = at(c * REST, OWN, LANES)
    theirs = at((1 - c) * REST, OWN, LANES)
    give = at(c * LANES, REST, LANES)
    rest = at((1 - c) * OWN, REST, LANES)
    owner = z < OWNERS
    zc = cols(jnp.minimum(z, OWNERS - 1))
    sources = [(z + NZ - d) % NZ < OWNERS for d in ring_z]

    def deal_out(value, src, dst):
        for q in range(NY):
            src[q] = value[:, q * 160 : (q + 1) * 160].astype(BF16)
        dst[y] = src[y]
        return [send(src.at[p], dst.at[y], device) for p, device in to_y]

    def core_sum(whole, other):
        return (whole[:, :, mine].astype(F32) + other[...].astype(F32)).astype(BF16)

    def flat(ref):
        return ref.reshape(ref.shape[0] * ref.shape[1], ref.shape[2])

    def chain(t, offset, r):
        part = pl.ds(offset, r)
        z_first = offset in Z_FIRST
        t.ax[x] = dot_back(s.pf[y, part, :], s.wi[...]).astype(BF16)
        a_x = spread(t.ax.at[x], to_x)
        yield
        arrive(a_x)
        t.a1[...] = in_order(t.ax).astype(BF16)
        a_c = send(t.a1, t.a2, to_c)
        yield
        arrive([a_c])
        gelu_value, gelu_slope = gelu_parts(t.a1[...].astype(F32) + t.a2[...].astype(F32))
        if offset == 0:
            arrive(wo_y)
        t.ms[...] = dot(gelu_value.astype(BF16), s.wo[...]).astype(BF16)
        m_z = scatter_cols(t.ms, t.mz)
        t.slope[...] = gelu_slope
        t.h_y = deal_out(gelu_value, t.hs, t.hr)
        yield
        arrive(m_z)
        t.m1[...] = total(t.ms[:, cols(z)], t.mz).astype(BF16)
        t.mf[y, :, cols(z)] = t.m1[...]
        near, far = (to_z, to_y) if z_first else (to_y, to_z)
        m_near = [send(t.m1, t.mf.at[y, :, cols(z)], device) for _, device in near]
        yield
        arrive(m_near)
        m_far = spread(t.mf.at[y] if z_first else t.mf.at[:, :, cols(z)], far)
        yield
        arrive(m_far)

        def project(weight, out):
            def tile(start, size):
                flat(out)[:, pl.ds(start, size)] = dot(flat(t.mf)[...], weight[:, pl.ds(start, size)]).astype(BF16)

            tiles(896, tile)

        project(s.wg, t.gp)
        g_c = send(t.gp.at[:, :, theirs], t.gc, to_c)
        project(s.wu, t.up)
        u_c = send(t.up.at[:, :, theirs], t.uc, to_c)
        yield
        arrive([g_c])
        t.gu[:, :, :OWN] = core_sum(t.gp, t.gc)
        arrive([u_c])
        t.gu[:, :, OWN:] = core_sum(t.up, t.uc)
        gu_x = scatter_blocks(t.gu, t.gux, to_x)
        yield
        arrive(gu_x)
        sums = total(t.gu[x], t.gux)
        hidden, gate_in, up_in = swiglu_backward(sums[:, :OWN], sums[:, OWN:], s.dsum[part, :])
        t.io[x, :, :OWN] = gate_in
        t.io[x, :, OWN:] = up_in
        io_x = spread(t.io.at[x], to_x)
        t.hdo[x] = hidden
        yield
        arrive(io_x)
        gi_c = [send(t.io.at[:, :, give], t.gir, to_c)]
        ui_c = [send(t.io.at[:, :, at(OWN + c * LANES, REST, LANES)], t.uir, to_c)]
        yield
        arrive(gi_c)
        arrive(ui_c)
        b_y = []
        for k in range(4):
            tile = pl.ds(k * 256, 256)
            flat(t.bp)[:, tile] = (
                dot_back(flat(t.io)[:, :OWN], s.wg[tile, mine])
                + dot_back(flat(t.io)[:, OWN:], s.wu[tile, mine])
                + dot_back(flat(t.gir)[...], s.wg[tile, rest])
                + dot_back(flat(t.uir)[...], s.wu[tile, rest])
            ).astype(BF16)
            b_y += scatter_blocks(t.bp, t.by, to_y, tile)
        hd_x = spread(t.hdo.at[x], to_x)
        yield
        arrive(b_y)
        t.bs[...] = total(t.bp[y], t.by).astype(BF16)
        b_z = scatter_cols(t.bs, t.bz)
        arrive(hd_x)
        t.hd_c = [send(t.hdo.at[:, :, give], t.hdr, to_c)]
        yield
        arrive(b_z)
        t.b1[...] = (s.of[y, part, cols(z)].astype(F32) + total(t.bs[:, cols(z)], t.bz)).astype(BF16)
        t.bf[y, :, cols(z)] = t.b1[...]
        b_gz = [send(t.b1, t.bf.at[y, :, cols(z)], device) for _, device in to_z]
        yield
        arrive(b_gz)
        t.cx[x] = dot_back(t.bf[y], s.wo[...]).astype(BF16)
        c_x = spread(t.cx.at[x], to_x)
        t.b_gy = spread(t.bf.at[y], to_y)
        yield
        arrive(c_x)
        t.c1[...] = in_order(t.cx).astype(BF16)
        c_c = send(t.c1, t.c2, to_c)
        yield
        arrive([c_c])
        pre_grad = (t.c1[...].astype(F32) + t.c2[...].astype(F32)) * t.slope[...]
        t.pg[...] = pre_grad.astype(BF16)
        t.qs[...] = dot(t.pg[...], s.wi[...]).astype(BF16)
        q_z = [
            (p, plan(t.qs.at[:, cols(jnp.minimum(p, OWNERS - 1))], t.qz.at[k], device)) for k, (p, device) in enumerate(to_z)
        ]
        for p, copy in q_z:
            pl.when(p < OWNERS)(copy.start)
        t.g_y = deal_out(pre_grad, t.gs, t.gr)
        yield
        q_near = [plan(t.q1, s.qf.at[y, part, zc], device) for _, device in near]

        @pl.when(owner)
        def _():
            for _, copy in q_z:
                copy.wait_recv()
            t.q1[...] = total(t.qs[:, zc], t.qz).astype(BF16)
            s.qf[y, part, zc] = t.q1[...]
            for copy in q_near:
                copy.start()

        yield
        if z_first:
            for copy, sends in zip(q_near, sources):
                pl.when(sends)(copy.wait_recv)
            q_far = spread(s.qf.at[y, part], far)
        else:
            q_far = [plan(s.qf.at[:, part, zc], s.qf.at[:, part, zc], device) for _, device in far]

            @pl.when(owner)
            def _():
                arrive(q_near)
                for copy in q_far:
                    copy.start()

        yield
        if z_first:
            arrive(q_far)
        else:
            for copy, sends in zip(q_far, sources):
                pl.when(sends)(copy.wait_recv)
        for p, copy in q_z:
            pl.when(p < OWNERS)(copy.wait_send)

        @pl.when(owner)
        def _():
            for copy in q_near if z_first else q_near + q_far:
                copy.wait_send()

    def wo_on():
        arrive(o_z)
        s.of[y] = dot(pick, s.oz[...]).astype(BF16)
        wo_y[:] = pass_on(s.wo, wo_y)

    def grads_y():
        o_y.extend(spread(s.of.at[y], to_y))
        loads["wd"].wait()

    def down():
        def tile(start, size):
            flat(s.dp)[:, pl.ds(start, size)] = dot_back(flat(s.of)[...], s.wd[pl.ds(start, size), :]).astype(BF16)

        arrive(o_y)
        tiles(896, tile)
        d_c.append(send(s.dp.at[:, :, theirs], s.dc, to_c))
        loads["wg"].wait()
        loads["wu"].wait()

    def down_x():
        arrive(d_c)
        s.d1[...] = core_sum(s.dp, s.dc)
        d_x.extend(scatter_blocks(s.d1, s.dx, to_x))

    def down_sum():
        p_y.extend(spread(s.pf.at[y], to_y))
        arrive(d_x)
        s.dsum[...] = total(s.d1[x], s.dx)

    def by_token(pairs):
        value = 0.0
        for left, right in pairs:
            value = value + dot_tokens(left, right)
        return value.astype(BF16)

    def weight_grad(out, own, other):
        def tile(start, size):
            lefts = [flat(t.mf)[:, pl.ds(start, size)] for t in halves_of]
            out[pl.ds(start, size), mine] = by_token([(a, flat(t.io)[:, own]) for a, t in zip(lefts, halves_of)])
            out[pl.ds(start, size), rest] = by_token([(a, flat(getattr(t, other))[...]) for a, t in zip(lefts, halves_of)])

        tiles(1024, tile)

    def down_grad():
        for t in halves_of:
            arrive(t.hd_c)

        def tile(start, size):
            tile_cols = pl.ds(start, size)
            rights = [s.of[:, pl.ds(o, r), tile_cols].reshape(NY * r, size) for o, r in PARTS]
            s.dg[mine, tile_cols] = by_token([(flat(t.hdo)[...], b) for t, b in zip(halves_of, rights)])
            s.dg[rest, tile_cols] = by_token([(flat(t.hdr)[...], b) for t, b in zip(halves_of, rights)])

        tiles(1024, tile)

    def outer_grad():
        for t in halves_of:
            arrive(t.h_y)
            arrive(t.b_gy)
        s.og[...] = by_token([(flat(t.hr)[...], flat(t.bf)[...]) for t in halves_of])

    def inner_grad():
        arrive(p_y)
        for t in halves_of:
            arrive(t.g_y)
        s.ig[...] = by_token([(flat(t.gr)[...], s.pf[:, pl.ds(o, r), :].reshape(NY * r, 640)) for t, (o, r) in zip(halves_of, PARTS)])

    o_y, p_y, d_c, d_x = [], [], [], []
    sent = []
    beside = {
        0: wo_on, 2: grads_y, 4: down, 5: down_x, 6: down_sum,
        9: lambda: weight_grad(s.gg, pl.ds(0, OWN), "gir"), 10: lambda: weight_grad(s.ug, pl.ds(OWN, OWN), "uir"), 11: down_grad,
        14: outer_grad, 15: inner_grad,
    }
    chains = [chain(t, o, r) for t, (o, r) in zip(halves_of, PARTS)]
    for step in range(18):
        for steps in chains:
            next(steps, None)
        if step in beside:
            beside[step]()
        sent.append(list(started))
        started.clear()
        if step >= 3:
            for wait_send in sent[step - 3]:
                wait_send()

    for wait_send in sum(sent[-3:], []):
        wait_send()


def local(patches, merge_inner, merge_outer, gate_weight, up_weight, down_weight, out_grad):
    vmem = pl.BlockSpec(memory_space=pltpu.VMEM)
    in_hbm = pl.BlockSpec(memory_space=pltpu.HBM)
    shapes = [(NY, ROWS, 640), (160, 640), (160, 1024), (1024, 896), (1024, 896), (896, 1024)]
    buffers = [*SCRATCH.values(), *(b for _, r in PARTS for b in part_scratch(r).values())]
    arrays = (patches, out_grad, merge_inner.T, merge_outer, gate_weight, up_weight, down_weight)
    results = pl.pallas_call(
        kernel,
        out_shape=[pltpu.VMEM(shape, BF16) for shape in shapes],
        in_specs=[in_hbm] * 7,
        out_specs=[vmem] * 6,
        scratch_shapes=[pltpu.VMEM(shape, dtype) for shape, dtype in buffers]
        + [pltpu.SemaphoreType.DMA((SEMS,)), pltpu.SemaphoreType.DMA((SEMS,)), pltpu.SemaphoreType.DMA((16,))],
        compiler_params=pltpu.CompilerParams(collective_id=0, has_side_effects=True, vmem_limit_bytes=56 * 2**20),
        name="layer",
    )(*(pltpu.with_memory_space_constraint(a, pltpu.HBM) for a in arrays))
    patch_grad, inner_grad, *others = results
    return (patch_grad.reshape(320, 640), inner_grad.T, *others)


def solution(mesh):
    in_specs = (
        P(("gy", "gz"), "gx"),
        P("gx", ("gy", "gz")),
        P(("gy", "gz"), "gx"),
        P("gx", ("gy", "gz")),
        P("gx", ("gy", "gz")),
        P(("gy", "gz"), "gx"),
        P(("gy", "gz"), "gx"),
    )
    out_specs = (
        P(None, "gx"),
        P("gx", ("gy", "gz")),
        P(("gy", "gz"), "gx"),
        P("gx", ("gy", "gz")),
        P("gx", ("gy", "gz")),
        P(("gy", "gz"), "gx"),
    )
    return jax.shard_map(local, mesh=mesh, in_specs=in_specs, out_specs=out_specs, check_vma=False)
```

profile of v0, /device:TPU:6, one launch (start us, length us, event | category | flops | bytes accessed | tf_op | source)
XLA Modules:
  0.0 121.3 jit_solution(6247666851706185268)
XLA Ops:
  0.6 114.9 %layer.1 = (bf16[4,80,640]{2,1,0:T(8,128)(2,1)S(1)}, bf16[160,640]{1,0:T(8,128)(2,1)S(1)}, bf16[160,1024]{1,0:T(8,128)(2,1)S(1)}, bf16[1024,896]{1,0:T(8,128)(2,...) custom-call(bf16[10,640]{1,0:T(8,128)(2,1)} %refs_0_.1, bf16[10,1024]{1,0:T(8,128)(2,1)} %refs_1_.1, ...), custom_call_target="tpu_custom_call" | custom-call | tf_op jit(solution)/shard_map/layer/pallas_call | solution.py:467
  115.5 0.8 copy.19
  116.3 0.7 copy.20
  116.9 0.7 copy.21
  117.7 1.2 %copy.22 = bf16[1024,896]{1,0:T(8,128)(2,1)} copy(bf16[1024,896]{1,0:T(8,128)(2,1)S(1)} %get-tuple-element.21) | data formatting | bytes 3670016
  118.9 1.2 %copy.23 = bf16[1024,896]{1,0:T(8,128)(2,1)} copy(bf16[1024,896]{1,0:T(8,128)(2,1)S(1)} %get-tuple-element.22) | data formatting | bytes 3670016
  120.1 1.2 %copy.24 = bf16[896,1024]{1,0:T(8,128)(2,1)} copy(bf16[896,1024]{1,0:T(8,128)(2,1)S(1)} %get-tuple-element.23) | data formatting | bytes 3670016
where the time goes:
time: 121 us
  Pallas kernels  115 us (95%)
  local copies, waits for them, and re-layouts  5.84 us (5%)
    pallas_call x1, Pallas kernels, local(): pl.pallas_call(kernel, out_shape=[pltpu.VMEM(shape, BF16) for shape in sh...  115 us
    unnamed x6, local copies, waits for them, and re-layouts  5.84 us

commit v1 on v0

--- a/solution.py
+++ b/solution.py
@@ -47,7 +47,7 @@
 
 
 SCRATCH = dict(
-    wi=((640, 640), BF16), wo=((640, 1024), BF16), wg=((1024, 896), BF16), wu=((1024, 896), BF16), wd=((896, 1024), BF16),
+    wi=((640, 640), BF16), wo=((640, 1024), BF16), wot=((1024, 640), BF16), wg=((1024, 896), BF16), wu=((1024, 896), BF16), wd=((896, 1024), BF16),
     p10=((10, 640), BF16), o10=((10, 1024), BF16), pp=((16, 640), BF16), op=((16, 1024), BF16),
     pz=((128, 640), BF16), oz=((128, 1024), BF16), pf=((NY, ROWS, 640), BF16), of=((NY, ROWS, 1024), BF16),
     dp=((NX, ROWS, 896), BF16), dc=((NX, ROWS, OWN), BF16), d1=((NX, ROWS, OWN), BF16), dx=((3, ROWS, OWN), BF16),
@@ -98,7 +98,7 @@
     x, c = gx // 2, gx % 2
     y, z = gy // 2, (gy % 2) * 4 + gz
     ring = (2, 1, 3)
-    ring_z = (4, 3, 5, 2, 6, 1, 7)
+    ring_z = (4, 5, 3, 6, 2, 7, 1)
     to_y = [((y + d) % NY, (gx, ((y + d) % NY) * 2 + z // 4, gz)) for d in ring]
     to_x = [((x + d) % NX, (((x + d) % NX) * 2 + c, gy, gz)) for d in ring]
     to_z = [((z + d) % NZ, (gx, y * 2 + ((z + d) % NZ) // 4, ((z + d) % NZ) % 4)) for d in ring_z]
@@ -310,7 +310,7 @@
         b_gz = [send(t.b1, t.bf.at[y, :, cols(z)], device) for _, device in to_z]
         yield
         arrive(b_gz)
-        t.cx[x] = dot_back(t.bf[y], s.wo[...]).astype(BF16)
+        t.cx[x] = dot(t.bf[y], s.wot[...]).astype(BF16)
         c_x = spread(t.cx.at[x], to_x)
         t.b_gy = spread(t.bf.at[y], to_y)
         yield
@@ -397,6 +397,9 @@
         arrive(d_x)
         s.dsum[...] = total(s.d1[x], s.dx)
 
+    def turn_outer():
+        s.wot[...] = s.wo[...].T
+
     def by_token(pairs):
         value = 0.0
         for left, right in pairs:
@@ -438,7 +441,7 @@
     o_y, p_y, d_c, d_x = [], [], [], []
     sent = []
     beside = {
-        0: wo_on, 2: grads_y, 4: down, 5: down_x, 6: down_sum,
+        0: wo_on, 2: grads_y, 4: down, 5: down_x, 6: down_sum, 7: turn_outer,
         9: lambda: weight_grad(s.gg, pl.ds(0, OWN), "gir"), 10: lambda: weight_grad(s.ug, pl.ds(OWN, OWN), "uir"), 11: down_grad,
         14: outer_grad, 15: inner_grad,
     }

time: 121 us -> 121 us (level)
  no operation moved by 1% of the time
where the time goes in v1:
time: 121 us
  Pallas kernels  115 us (95%)
  local copies, waits for them, and re-layouts  5.84 us (5%)
    pallas_call x1, Pallas kernels, local(): pl.pallas_call(kernel, out_shape=[pltpu.VMEM(shape, BF16) for shape in sh...  115 us
    unnamed x6, local copies, waits for them, and re-layouts  5.84 us

profile of v1, /device:TPU:6, one launch (start us, length us, event | category | flops | bytes accessed | tf_op | source)
XLA Modules:
  0.0 121.1 jit_solution(3808507304137940163)
XLA Ops:
  0.6 114.7 %layer.1 = (bf16[4,80,640]{2,1,0:T(8,128)(2,1)S(1)}, bf16[160,640]{1,0:T(8,128)(2,1)S(1)}, bf16[160,1024]{1,0:T(8,128)(2,1)S(1)}, bf16[1024,896]{1,0:T(8,128)(2,...) custom-call(bf16[10,640]{1,0:T(8,128)(2,1)} %refs_0_.1, bf16[10,1024]{1,0:T(8,128)(2,1)} %refs_1_.1, ...), custom_call_target="tpu_custom_call" | custom-call | tf_op jit(solution)/shard_map/layer/pallas_call | solution.py:470
  115.3 0.8 copy.19
  116.0 0.7 copy.20
  116.7 0.7 copy.21
  117.5 1.2 %copy.22 = bf16[1024,896]{1,0:T(8,128)(2,1)} copy(bf16[1024,896]{1,0:T(8,128)(2,1)S(1)} %get-tuple-element.21) | data formatting | bytes 3670016
  118.7 1.2 %copy.23 = bf16[1024,896]{1,0:T(8,128)(2,1)} copy(bf16[1024,896]{1,0:T(8,128)(2,1)S(1)} %get-tuple-element.22) | data formatting | bytes 3670016
  119.9 1.2 %copy.24 = bf16[896,1024]{1,0:T(8,128)(2,1)} copy(bf16[896,1024]{1,0:T(8,128)(2,1)S(1)} %get-tuple-element.23) | data formatting | bytes 3670016
